TPU v7x, 32 devices: a whole 2x2x4 slice. The times are simulated.
32 devices in a mesh: ctx: 8 (over y, x, core), exp: 4 (over z).
Axes of the slice: x: 2, y: 2, z: 4, core: 2. Of those that a mesh axis runs over, the one named last changes fastest.
Arguments:
- inputs: bfloat16 [1024, 1024], P('exp', 'ctx'), may hold values from -6 to 6
- conv_taps: float32 [1024, 31], P('exp'), may hold values from -1 to 1
- norm_gain: bfloat16 [1024], P('exp'), may hold values from 0.099609375 to 1.8984375
- routes: int32 [1024, 2], P('ctx'), may hold values from 0 to 7, all different within a row; in each aligned block of 128 rows (0 to 127, 128 to 255, ...) at most 32 rows name the same one
- gate_probs: float32 [1024, 2], P('ctx'), may hold values from 0.1 to 0.9
- w_gate: bfloat16 [8, 1024, 4096], P('ctx', None, 'exp'), may hold values from -0.1875 to 0.1875
- w_up: bfloat16 [8, 1024, 4096], P('ctx', None, 'exp'), may hold values from -0.1875 to 0.1875
- w_down: bfloat16 [8, 4096, 1024], P('ctx', 'exp'), may hold values from -0.09375 to 0.09375
- grad_out: bfloat16 [1024, 1024], P('exp', 'ctx'), may hold values from -6 to 6
Outputs:
- layer_out: bfloat16 [1024, 1024], P('exp', 'ctx')
- grad_inputs: bfloat16 [1024, 1024], P('exp', 'ctx')
- grad_taps: float32 [1024, 31], P('exp')
- grad_gain: float32 [1024], P('exp')
- grad_gates: float32 [1024, 2], P('ctx')
- grad_w_gate: bfloat16 [8, 1024, 4096], P('ctx', None, 'exp')
- grad_w_up: bfloat16 [8, 1024, 4096], P('ctx', None, 'exp')
- grad_w_down: bfloat16 [8, 4096, 1024], P('ctx', 'exp')
Inputs may be any that keep to these rules, and one draw needn't show every extreme that they name: `routes`: in each aligned block of 128 rows (the rows of one index of ctx) no expert is named by more than 32 rows, a bound that some block reaches; the two experts of a row differ.
All inputs are finite; a program needn't handle non-finite values.
Results may differ from a plain program's by a relative error of at most 0.025.
Values may be sent and summed in bfloat16 or wider, within the bound.
A program may use at most 64 MiB of HBM per device.

v0:
```python
import jax
import jax.numpy as jnp
from jax import lax
from jax.sharding import PartitionSpec as P

EPS = 1e-05


def padded_2(cells, sides, width):
    for axis, dim in sides:
        count = lax.axis_size(axis)
        head = lax.slice_in_dim(cells, 0, width, axis=dim)
        tail = lax.slice_in_dim(cells, cells.shape[dim] - width, cells.shape[dim], axis=dim)
        cells = jnp.concatenate(
            [
                lax.ppermute(tail, axis, [(i, (i + 1) % count) for i in range(count)]),
                cells,
                lax.ppermute(head, axis, [((i + 1) % count, i) for i in range(count)]),
            ],
            axis=dim,
        )
    return cells


def shortened(x):

    def short(part):
        return part.astype(jnp.bfloat16) if part.dtype == jnp.float32 else part

    return jax.tree.map(short, x)


def slot_rows(routes, experts, capacity):
    flat = routes.reshape(-1)
    onehot = (flat[:, None] == jnp.arange(experts, dtype=jnp.int32)[None, :]).astype(jnp.int32)
    before = jnp.cumsum(onehot, axis=0, dtype=jnp.int32) - onehot
    place = jnp.sum(before * onehot, axis=1, dtype=jnp.int32)
    return flat * capacity + place


def bring_back(values, dest, weights, experts, capacity, whole_cot):
    width = values.shape[1]
    back = lax.all_to_all(
        values.reshape(experts, capacity, width).astype(jnp.bfloat16),
        "ctx",
        split_axis=0,
        concat_axis=0,
        tiled=True,
    ).astype(jnp.float32)
    picked = back.reshape(experts * capacity, width)[dest]
    term = jnp.sum((picked * weights[:, None]).reshape(-1, 2, width), axis=1)
    share = lax.psum_scatter(
        term.astype(jnp.bfloat16), "exp", scatter_dimension=1, tiled=True
    ).astype(jnp.float32)
    dots = None if whole_cot is None else jnp.sum(picked * whole_cot, axis=1)
    return (share, dots)


def local(inputs, conv_taps, norm_gain, routes, gate_probs, w_gate, w_up, w_down, grad_out):
    chans, tokens = inputs.shape
    taps = conv_taps.shape[1]
    half = taps // 2
    width = w_gate.shape[1]
    experts = lax.axis_size("ctx")
    capacity = max(tokens // 8, (2 * tokens + experts - 1) // experts)
    padded = padded_2(inputs, (("ctx", 1),), half)
    padded_f = padded.astype(jnp.float32)
    conv = jnp.zeros((chans, tokens), jnp.float32)
    for offset in range(taps):
        conv = conv + conv_taps[:, offset : offset + 1] * padded_f[:, offset : offset + tokens]
    mixed = (inputs.astype(jnp.float32) + conv).astype(jnp.bfloat16)
    mixed_f = mixed.astype(jnp.float32)
    gain_f = norm_gain.astype(jnp.float32)
    squares = lax.psum(jnp.sum(mixed_f * mixed_f, axis=0), "exp")
    scale = lax.rsqrt(squares / width + EPS)
    normed_part = (mixed_f * gain_f[:, None] * scale[None, :]).astype(jnp.bfloat16)
    normed, cotangent = (
        lax.all_gather(normed_part, "exp", axis=0, tiled=True),
        lax.all_gather(grad_out, "exp", axis=0, tiled=True),
    )
    dest = slot_rows(routes, experts, capacity)
    gates = gate_probs.reshape(-1)
    cot_rows = jnp.repeat(cotangent.T, 2, axis=0).astype(jnp.float32)
    token_rows = jnp.repeat(normed.T, 2, axis=0)
    scaled_rows = (cot_rows * gates[:, None]).astype(jnp.bfloat16)
    empty = jnp.zeros((experts * capacity, width), jnp.bfloat16)
    send_x = empty.at[dest].set(token_rows).reshape(experts, capacity, width)
    send_dy = empty.at[dest].set(scaled_rows).reshape(experts, capacity, width)
    recv_x, recv_dy = (
        lax.all_to_all(send_x, "ctx", split_axis=0, concat_axis=0, tiled=True),
        lax.all_to_all(send_dy, "ctx", split_axis=0, concat_axis=0, tiled=True),
    )
    rows_x = recv_x.reshape(-1, width)
    rows_dy = recv_dy.reshape(-1, width)
    weight_gate = w_gate[0]
    weight_up = w_up[0]
    weight_down = w_down[0]
    gate_act = jnp.dot(rows_x, weight_gate, preferred_element_type=jnp.float32)
    up_act = jnp.dot(rows_x, weight_up, preferred_element_type=jnp.float32)
    sigma = jax.nn.sigmoid(gate_act)
    hidden = (gate_act * sigma * up_act).astype(jnp.bfloat16)
    partial_out = jnp.dot(hidden, weight_down, preferred_element_type=jnp.float32)
    moe_share, gate_dots = bring_back(partial_out, dest, gates, experts, capacity, cot_rows)
    layer_out = (mixed_f + moe_share.T).astype(jnp.bfloat16)
    grad_gates = lax.psum(gate_dots, "exp").reshape(tokens, 2)
    contract_last = (((1,), (1,)), ((), ()))
    contract_first = (((0,), (0,)), ((), ()))
    d_hidden = lax.dot_general(
        rows_dy, weight_down, contract_last, preferred_element_type=jnp.float32
    )
    grad_down = lax.dot_general(
        hidden, rows_dy, contract_first, preferred_element_type=jnp.float32
    ).astype(jnp.bfloat16)
    d_gate = (d_hidden * up_act * sigma * (1.0 + gate_act * (1.0 - sigma))).astype(jnp.bfloat16)
    d_up = (d_hidden * gate_act * sigma).astype(jnp.bfloat16)
    grad_gate = lax.dot_general(
        rows_x, d_gate, contract_first, preferred_element_type=jnp.float32
    ).astype(jnp.bfloat16)
    grad_up = lax.dot_general(
        rows_x, d_up, contract_first, preferred_element_type=jnp.float32
    ).astype(jnp.bfloat16)
    d_rows = lax.dot_general(d_gate, weight_gate, contract_last, preferred_element_type=jnp.float32)
    d_rows = d_rows + lax.dot_general(
        d_up, weight_up, contract_last, preferred_element_type=jnp.float32
    )
    d_share, unused_dots = bring_back(d_rows, dest, jnp.ones_like(gates), experts, capacity, None)
    d_normed = d_share.T
    gain_local = jnp.sum(d_normed * mixed_f * scale[None, :], axis=1)
    norm_terms = lax.psum(jnp.sum(d_normed * gain_f[:, None] * mixed_f, axis=0), "exp")
    cot_own = grad_out.astype(jnp.float32)
    d_mixed = (
        cot_own
        + gain_f[:, None] * d_normed * scale[None, :]
        - mixed_f * (norm_terms * scale * scale * scale / width)[None, :]
    )
    grad_padded = padded_2(shortened(d_mixed), (("ctx", 1),), half).astype(d_mixed.dtype)
    grad_in = d_mixed
    tap_parts = []
    for offset in range(taps):
        grad_in = (
            grad_in
            + conv_taps[:, offset : offset + 1]
            * grad_padded[:, 2 * half - offset : 2 * half - offset + tokens]
        )
        tap_parts.append(jnp.sum(d_mixed * padded_f[:, offset : offset + tokens], axis=1))
    tap_local = jnp.stack(tap_parts, axis=1)
    grad_taps, grad_gain = lax.psum((tap_local, gain_local), "ctx")
    return (
        layer_out,
        grad_in.astype(jnp.bfloat16),
        grad_taps,
        grad_gain,
        grad_gates,
        grad_gate[None],
        grad_up[None],
        grad_down[None],
    )


def solution(mesh):
    return jax.shard_map(
        local,
        mesh=mesh,
        in_specs=(
            P("exp", "ctx"),
            P("exp", None),
            P("exp"),
            P("ctx", None),
            P("ctx", None),
            P("ctx", None, "exp"),
            P("ctx", None, "exp"),
            P("ctx", "exp", None),
            P("exp", "ctx"),
        ),
        out_specs=(
            P("exp", "ctx"),
            P("exp", "ctx"),
            P("exp", None),
            P("exp"),
            P("ctx", None),
            P("ctx", None, "exp"),
            P("ctx", None, "exp"),
            P("ctx", "exp", None),
        ),
        check_vma=False,
    )
```

profile of v0, /device:TPU:0, one launch (start us, length us, event | category | flops | bytes accessed | tf_op | source)
XLA Modules:
  0.0 213.7 jit_solution(18306011151170475799)
XLA Ops:
  7.2 1.1 copy.28
  8.3 0.5 collective-permute-start
  8.8 2.9 %collective-permute-start.1 = (bf16[256,15]{0,1:T(8,128)(2,1)S(1)}, bf16[256,15]{0,1:T(8,128)(2,1)S(1)}, u32[]{:S(2)}, u32[]{:S(2)}) collective-permute-start(bf16[256,15]{0,1:T(8,128)(2,1)S(1)} %get-tuple-element.72), channel_id=1, source_target_pairs={{4,0},{8,4},{12,8},{16,12},{20,16},{24,20},{28,24},{0,28},{5,1},{9... | collective-permute-start | bytes 23048 | tf_op jit(solution)/shard_map/ppermute | solution.py:18
  11.7 0.7 broadcast_multiply_fusion
  12.4 0.8 copy.33
  13.2 0.1 eq.29
  13.3 0.1 eq.25
  13.6 0.1 mul.817
  13.7 0.8 copy.35
  14.5 0.1 mul.828
  14.7 0.6 reduce-window.6
  15.3 0.2 slice_reduce_fusion
  15.5 15.0 %all_gather.7 = bf16[1024,128]{1,0:T(8,128)(2,1)S(1)} all-gather(bf16[256,128]{1,0:T(8,128)(2,1)} %param.17), channel_id=1, replica_groups=mesh['ctx'=8,'exp'=4] {'exp'}, dimensions={0}, use_global_device_ids=true | all-gather | bytes 327680 | tf_op jit(solution)/shard_map/all_gather | solution.py:79
  30.6 0.2 copy.37
  30.8 1.3 broadcast_in_dim.14
  32.1 1.9 convert_element_type.108
  34.2 2.5 %scatter_custom_fusion.1 = bf16[256,1024]{1,0:T(8,128)(2,1)} fusion(s32[256]{0:T(256)S(1)} %bitcast.245, f32[256,1024]{1,0:T(8,128)S(1)} %convert_element_type.108, f32[256]{0:T(256)S(1)} %mul.828, bf16[]{:T(256)} %constant.8.clone.1), kind=kCustom, calls=%fused_computation.29 | custom fusion | flops 524288 | bytes 1573890 | tf_op jit(solution)/shard_map/scatter | solution.py:88
  36.7 4.1 %all-to-all-start.2 = ((bf16[8,32,1024]{2,1,0:T(8,128)(2,1)}), bf16[8,32,1024]{2,1,0:T(8,128)(2,1)}, u32[]{:S(2)}, u32[]{:S(2)}) async-start(bf16[8,32,1024]{2,1,0:T(8,128)(2,1)} %bitcast.149), calls=%async_computation.3 | async-start | bytes 1048576 | tf_op jit(solution)/shard_map/all_to_all | solution.py:91
  41.2 1.0 fusion.28
  42.4 11.9 %psum.35 = f32[128]{0:T(128)S(1)} all-reduce(f32[128]{0:T(128)} %get-tuple-element.62), channel_id=1, replica_groups=mesh['ctx'=8,'exp'=4] {'exp'}, use_global_device_ids=true, to_apply=%region_4.5 | all-reduce | flops 128 | bytes 1024 | tf_op jit(solution)/shard_map/psum | solution.py:74
  54.3 0.5 copy-done.64
  54.9 13.8 %all_gather.6 = bf16[1024,128]{0,1:T(8,128)(2,1)S(1)} all-gather(bf16[256,128]{0,1:T(8,128)(2,1)S(1)} %fusion.27), channel_id=1, replica_groups=mesh['ctx'=8,'exp'=4] {'exp'}, dimensions={0}, use_global_device_ids=true | all-gather | bytes 327680 | tf_op jit(solution)/shard_map/all_gather | solution.py:78
  68.7 0.3 broadcast_in_dim.13
  69.0 0.2 reshape.158
  69.2 2.6 %scatter_custom_fusion = bf16[256,1024]{1,0:T(8,128)(2,1)} fusion(s32[256]{0:T(256)} %bitcast.246, bf16[256,1024]{1,0:T(8,128)(2,1)S(1)} %reshape.158, bf16[]{:T(256)} %constant.8.clone.1), kind=kCustom, calls=%fused_computation.41 | custom fusion | bytes 524800 | tf_op jit(solution)/shard_map/scatter | solution.py:87
  71.8 4.1 %all-to-all-start = ((bf16[8,32,1024]{2,1,0:T(8,128)(2,1)}), bf16[8,32,1024]{2,1,0:T(8,128)(2,1)S(1)}, u32[]{:S(2)}, u32[]{:S(2)}) async-start(bf16[8,32,1024]{2,1,0:T(8,128)(2,1)} %bitcast.36), calls=%async_computation | async-start | bytes 1048576 | tf_op jit(solution)/shard_map/all_to_all | solution.py:90
  75.8 0.7 pad_clamp_fusion
  76.5 3.5 %fusion.2 = f32[256,1024]{1,0:T(8,128)} fusion(bf16[256,1024]{1,0:T(8,128)(2,1)} %bitcast.47, bf16[1,1024,1024]{2,1,0:T(8,128)(2,1)} %param.16), kind=kOutput, calls=%fused_computation.6 | convolution fusion | flops 536870912 | bytes 3670016 | tf_op jit(solution)/shard_map/dot_general | solution.py:108
  80.0 5.6 %all-to-all-done = bf16[8,32,1024]{2,1,0:T(8,128)(2,1)S(1)} async-done(((bf16[8,32,1024]{2,1,0:T(8,128)(2,1)}), bf16[8,32,1024]{2,1,0:T(8,128)(2,1)S(1)}, u32[]{:S(2)}, u32[]{:S(2)}) %all-to-all-start) | async-done | bytes 524320 | tf_op jit(solution)/shard_map/all_to_all | solution.py:90
  85.6 2.5 %fusion.6 = f32[256,1024]{1,0:T(8,128)S(1)} fusion(bf16[256,1024]{1,0:T(8,128)(2,1)S(1)} %bitcast.145, bf16[1,1024,1024]{2,1,0:T(8,128)(2,1)} %param.15), kind=kOutput, calls=%fused_computation.10 | convolution fusion | flops 536870912 | bytes 3670016 | tf_op jit(solution)/shard_map/dot_general | solution.py:99
  88.1 2.0 multiply_convert_fusion.1
  90.1 0.8 copy-done.14
  90.9 1.5 fusion.15
  92.5 3.5 %all-to-all-start.1 = ((bf16[8,32,1024]{2,1,0:T(8,128)(2,1)}), bf16[8,32,1024]{2,1,0:T(8,128)(2,1)S(1)}, u32[]{:S(2)}, u32[]{:S(2)}) async-start(bf16[8,32,1024]{2,1,0:T(8,128)(2,1)} %fusion.15), calls=%async_computation.1 | async-start | bytes 1048576 | tf_op jit(solution)/shard_map/all_to_all | solution.py:43
  96.0 2.4 %fusion.4 = f32[256,1024]{1,0:T(8,128)S(1)} fusion(bf16[256,1024]{1,0:T(8,128)(2,1)S(1)} %get-tuple-element.66, bf16[1,1024,1024]{2,1,0:T(8,128)(2,1)} %param.15), kind=kOutput, calls=%fused_computation.8 | convolution fusion | flops 536870912 | bytes 3670016 | tf_op jit(solution)/shard_map/dot_general | solution.py:123
  98.4 1.6 fusion.18
  100.0 5.7 %all-to-all-done.1 = bf16[8,32,1024]{2,1,0:T(8,128)(2,1)S(1)} async-done(((bf16[8,32,1024]{2,1,0:T(8,128)(2,1)}), bf16[8,32,1024]{2,1,0:T(8,128)(2,1)S(1)}, u32[]{:S(2)}, u32[]{:S(2)}) %all-to-all-start.1) | async-done | bytes 524320 | tf_op jit(solution)/shard_map/all_to_all | solution.py:43
  105.6 4.2 %all-to-all-start.3 = ((bf16[8,32,1024]{2,1,0:T(8,128)(2,1)}), bf16[8,32,1024]{2,1,0:T(8,128)(2,1)}, u32[]{:S(2)}, u32[]{:S(2)}) async-start(bf16[8,32,1024]{2,1,0:T(8,128)(2,1)} %bitcast.48), calls=%async_computation.4 | async-start | bytes 1048576 | tf_op jit(solution)/shard_map/all_to_all | solution.py:43
  109.8 0.2 reduce-scatter.3.cloned.1.call-start
  110.0 1.1 bitcast_convert_fusion.1
  111.2 2.1 gather_fusion
  113.3 2.9 %gather.9 = f32[128,2,1024]{2,1,0:T(2,128)} reshape(f32[256,1024]{1,0:T(8,128)} %gather_fusion) | data formatting | bytes 2097152 | tf_op jit(solution)/shard_map/gather | solution.py:50
  116.2 3.3 %multiply_reduce_fusion.1 = bf16[128,1024]{1,0:T(8,128)(2,1)} fusion(f32[128,2,1024]{2,1,0:T(2,128)} %gather.9, f32[128,2]{1,0:T(8,128)S(1)} %copy.35), kind=kLoop, calls=%fused_computation.26 | loop fusion | flops 393216 | bytes 1311744 | tf_op jit(solution)/shard_map/reduce_sum | solution.py:51
  119.7 2.1 convert_bitcast_fusion.2
  121.8 1.1 bitcast_convert_fusion
  123.0 2.0 gather_fusion.1
  125.0 2.9 %reshape.132 = f32[128,2,1024]{2,1,0:T(2,128)} reshape(f32[256,1024]{1,0:T(8,128)} %gather_fusion.1) | data formatting | bytes 2097152 | tf_op jit(solution)/shard_map/reshape | solution.py:51
  127.9 3.2 %reduce_sum.348 = bf16[128,1024]{1,0:T(8,128)(2,1)} reduce(f32[128,2,1024]{2,1,0:T(2,128)} %reshape.132, f32[]{:T(128)} %constant.7.clone.1), dimensions={1}, to_apply=%region_9.10 | reduce | flops 131072 | bytes 1310724 | tf_op jit(solution)/shard_map/reduce_sum | solution.py:51
  131.1 2.1 convert_bitcast_fusion.1
  133.2 3.3 %convert_bitcast_fusion = bf16[1,1024,1024]{2,1,0:T(8,128)(2,1)} fusion(bf16[256,1024]{1,0:T(8,128)(2,1)S(1)} %copy-done.15, bf16[256,1024]{1,0:T(8,128)(2,1)} %bitcast.47), kind=kOutput, calls=%fused_computation.16 | convolution fusion | flops 537919488 | bytes 3145728 | tf_op jit(solution)/shard_map/dot_general | solution.py:111
  136.5 0.2 multiply_reduce_fusion
  136.7 0.1 reshape.133
  136.8 0.9 reduce-scatter.3.cloned.1.call-done
  137.8 20.4 %reduce-scatter.5.cloned.1.call-done = bf16[128,256]{1,0:T(8,128)(2,1)} async-done(((bf16[128,1024]{1,0:T(8,128)(2,1)}), bf16[128,256]{1,0:T(8,128)(2,1)}) %reduce-scatter.5.cloned.1.call-update) | async-done | bytes 65552 | tf_op jit(solution)/shard_map/reduce_scatter | solution.py:52
  158.1 1.0 fusion.33
  159.1 17.2 %all-reduce.1 = (f32[128]{0:T(128)S(1)}, f32[128,2]{1,0:T(8,128)S(1)}) all-reduce(f32[128]{0:T(128)S(1)} %get-tuple-element.56, f32[128,2]{1,0:T(8,128)S(1)} %reshape.133), channel_id=1, replica_groups=mesh['ctx'=8,'exp'=4] {'exp'}, use_global_device_ids=true, to_apply=%region_12.13 | all-reduce | flops 384 | bytes 3072 | tf_op jit(solution)/shard_map/psum | solution.py:129
  176.6 1.2 multiply_reduce_fusion.2
  177.8 0.2 multiply_reduce_fusion.20
  178.1 2.6 %collective-permute-start.3 = (bf16[256,15]{0,1:T(8,128)(2,1)S(1)}, bf16[256,15]{0,1:T(8,128)(2,1)S(1)}, u32[]{:S(2)}, u32[]{:S(2)}) collective-permute-start(bf16[256,15]{0,1:T(8,128)(2,1)S(1)} %get-tuple-element.69), channel_id=1, source_target_pairs={{4,0},{8,4},{12,8},{16,12},{20,16},{24,20},{28,24},{0,28},{5,1},{9... | collective-permute-start | bytes 23048 | tf_op jit(solution)/shard_map/ppermute | solution.py:18
  180.8 23.3 %all-reduce = (f32[256,31]{0,1:T(8,128)}, f32[256]{0:T(256)}) all-reduce(f32[256,31]{0,1:T(8,128)S(1)} %stack.127, f32[256]{0:T(256)S(1)} %get-tuple-element.55), channel_id=1, replica_groups=mesh['ctx'=8,'exp'=4] {'ctx'}, use_global_device_ids=true, to_apply=%region_44.45 | all-reduce | flops 8192 | bytes 65536 | tf_op jit(solution)/shard_map/psum | solution.py:147
  204.1 0.6 copy.41
  204.7 0.7 copy.39
  205.7 0.4 fusion.35
  206.1 0.7 copy.40
  (159 shorter events, 1.1 us)
Async XLA Ops:
  7.2 81.0 %copy-start = (bf16[1,1024,1024]{2,1,0:T(8,128)(2,1)S(1)}, bf16[1,1024,1024]{2,1,0:T(8,128)(2,1)}, u32[]{:S(2)}) copy-start(bf16[1,1024,1024]{2,1,0:T(8,128)(2,1)} %param.14) | copy-start | bytes 6291460
  8.3 32.8 %collective-permute-start = (bf16[256,15]{0,1:T(8,128)(2,1)S(1)}, bf16[256,15]{0,1:T(8,128)(2,1)S(1)}, u32[]{:S(2)}, u32[]{:S(2)}) collective-permute-start(bf16[256,15]{0,1:T(8,128)(2,1)S(1)} %get-tuple-element.71), channel_id=1, source_target_pairs={{0,4},{4,8},{8,12},{12,16},{16,20},{20,24},{24,28},{28,0},{1,5},{5... | collective-permute-start | bytes 23048 | tf_op jit(solution)/shard_map/ppermute | solution.py:16
  8.8 32.4 %collective-permute-start.1 = (bf16[256,15]{0,1:T(8,128)(2,1)S(1)}, bf16[256,15]{0,1:T(8,128)(2,1)S(1)}, u32[]{:S(2)}, u32[]{:S(2)}) collective-permute-start(bf16[256,15]{0,1:T(8,128)(2,1)S(1)} %get-tuple-element.72), channel_id=1, source_target_pairs={{4,0},{8,4},{12,8},{16,12},{20,16},{24,20},{28,24},{0,28},{5,1},{9... | collective-permute-start | bytes 23048 | tf_op jit(solution)/shard_map/ppermute | solution.py:18
  32.1 8.7 %copy-start.17 = (f32[256,31]{0,1:T(8,128)S(1)}, f32[256,31]{0,1:T(8,128)}, u32[]{:S(2)}) copy-start(f32[256,31]{0,1:T(8,128)} %param.10) | copy-start | bytes 95236
  32.1 8.9 %copy-start.63 = (bf16[256]{0:T(256)(128)(2,1)S(1)}, bf16[256]{0:T(256)(128)(2,1)}, u32[]{:S(2)}) copy-start(bf16[256]{0:T(256)(128)(2,1)} %param.11) | copy-start | bytes 1540
  34.1 8.1 %copy-start.2 = (f32[256,1024]{1,0:T(8,128)}, f32[256,1024]{1,0:T(8,128)S(1)}, u32[]{:S(2)}) copy-start(f32[256,1024]{1,0:T(8,128)S(1)} %convert_element_type.108) | copy-start | bytes 3145732
  34.2 7.0 %copy-start.62 = (s32[256,1]{0,1:T(1,128)}, s32[256,1]{0,1:T(1,128)S(1)}, u32[]{:S(2)}) copy-start(s32[256,1]{0,1:T(1,128)S(1)} %compare_select_fusion) | copy-start | bytes 3076
  36.7 35.1 %all-to-all-start.2 = ((bf16[8,32,1024]{2,1,0:T(8,128)(2,1)}), bf16[8,32,1024]{2,1,0:T(8,128)(2,1)}, u32[]{:S(2)}, u32[]{:S(2)}) async-start(bf16[8,32,1024]{2,1,0:T(8,128)(2,1)} %bitcast.149), calls=%async_computation.3 | async-start | bytes 1048576 | tf_op jit(solution)/shard_map/all_to_all | solution.py:91
  40.9 1.3 copy-start.18
  40.9 1.3 copy-start.20
  40.9 1.3 copy-start.22
  40.9 1.3 copy-start.24
  40.9 1.3 copy-start.26
  40.9 1.3 copy-start.28
  40.9 1.3 copy-start.30
  40.9 1.3 copy-start.32
  41.0 1.3 copy-start.34
  41.0 1.2 copy-start.36
  41.0 1.2 copy-start.38
  54.8 17.0 %copy-start.60 = (f32[128]{0:T(128)}, f32[128]{0:T(128)S(1)}, u32[]{:S(2)}) copy-start(f32[128]{0:T(128)S(1)} %add_rsqrt_fusion) | copy-start | bytes 1540
  71.8 13.8 %all-to-all-start = ((bf16[8,32,1024]{2,1,0:T(8,128)(2,1)}), bf16[8,32,1024]{2,1,0:T(8,128)(2,1)S(1)}, u32[]{:S(2)}, u32[]{:S(2)}) async-start(bf16[8,32,1024]{2,1,0:T(8,128)(2,1)} %bitcast.36), calls=%async_computation | async-start | bytes 1048576 | tf_op jit(solution)/shard_map/all_to_all | solution.py:90
  85.6 4.5 %copy-start.4 = (bf16[8,32,1024]{2,1,0:T(8,128)(2,1)}, bf16[8,32,1024]{2,1,0:T(8,128)(2,1)S(1)}, u32[]{:S(2)}) copy-start(bf16[8,32,1024]{2,1,0:T(8,128)(2,1)S(1)} %all-to-all-done) | copy-start | bytes 1572868
  85.6 2.5 %copy-start.13 = (f32[256,1024]{1,0:T(8,128)S(1)}, f32[256,1024]{1,0:T(8,128)}, u32[]{:S(2)}) copy-start(f32[256,1024]{1,0:T(8,128)} %fusion.2) | copy-start | bytes 3145732
  88.1 2.8 %copy-start.7 = (bf16[1,1024,1024]{2,1,0:T(8,128)(2,1)S(1)}, bf16[1,1024,1024]{2,1,0:T(8,128)(2,1)}, u32[]{:S(2)}) copy-start(bf16[1,1024,1024]{2,1,0:T(8,128)(2,1)} %param.16) | copy-start | bytes 6291460
  90.1 5.8 %copy-start.9 = (bf16[256,1024]{1,0:T(8,128)(2,1)}, bf16[256,1024]{1,0:T(8,128)(2,1)S(1)}, u32[]{:S(2)}) copy-start(bf16[256,1024]{1,0:T(8,128)(2,1)S(1)} %get-tuple-element.66) | copy-start | bytes 1572868
  92.5 13.2 %all-to-all-start.1 = ((bf16[8,32,1024]{2,1,0:T(8,128)(2,1)}), bf16[8,32,1024]{2,1,0:T(8,128)(2,1)S(1)}, u32[]{:S(2)}, u32[]{:S(2)}) async-start(bf16[8,32,1024]{2,1,0:T(8,128)(2,1)} %fusion.15), calls=%async_computation.1 | async-start | bytes 1048576 | tf_op jit(solution)/shard_map/all_to_all | solution.py:43
  96.0 2.4 %copy-start.11 = (bf16[256,1024]{1,0:T(8,128)(2,1)S(1)}, bf16[256,1024]{1,0:T(8,128)(2,1)}, u32[]{:S(2)}) copy-start(bf16[256,1024]{1,0:T(8,128)(2,1)} %get-tuple-element.64) | copy-start | bytes 1572868
  105.6 4.2 %copy-start.8 = (bf16[8,32,1024]{2,1,0:T(8,128)(2,1)}, bf16[8,32,1024]{2,1,0:T(8,128)(2,1)S(1)}, u32[]{:S(2)}) copy-start(bf16[8,32,1024]{2,1,0:T(8,128)(2,1)S(1)} %all-to-all-done.1) | copy-start | bytes 1572868
  105.6 16.2 %all-to-all-start.3 = ((bf16[8,32,1024]{2,1,0:T(8,128)(2,1)}), bf16[8,32,1024]{2,1,0:T(8,128)(2,1)}, u32[]{:S(2)}, u32[]{:S(2)}) async-start(bf16[8,32,1024]{2,1,0:T(8,128)(2,1)} %bitcast.48), calls=%async_computation.4 | async-start | bytes 1048576 | tf_op jit(solution)/shard_map/all_to_all | solution.py:43
  109.8 27.9 %reduce-scatter.3.cloned.1.call-start = ((), (), s32[]{:S(2)}) async-start(), calls=%async_computation.6 | async-start | bytes 327680 | tf_op jit(solution)/shard_map/reduce_scatter | solution.py:52
  113.3 6.3 %copy-start.16 = (bf16[256,128]{1,0:T(8,128)(2,1)S(1)}, bf16[256,128]{1,0:T(8,128)(2,1)}, u32[]{:S(2)}) copy-start(bf16[256,128]{1,0:T(8,128)(2,1)} %param.17) | copy-start | bytes 196612
  113.3 6.4 %copy-start.5 = (bf16[8,32,1024]{2,1,0:T(8,128)(2,1)S(1)}, bf16[8,32,1024]{2,1,0:T(8,128)(2,1)}, u32[]{:S(2)}) copy-start(bf16[8,32,1024]{2,1,0:T(8,128)(2,1)} %copy-done.4) | copy-start | bytes 1572868
  113.3 6.5 %copy-start.12 = (bf16[256,1024]{1,0:T(8,128)(2,1)S(1)}, bf16[256,1024]{1,0:T(8,128)(2,1)}, u32[]{:S(2)}) copy-start(bf16[256,1024]{1,0:T(8,128)(2,1)} %get-tuple-element.64) | copy-start | bytes 1572868
  119.6 38.6 %reduce-scatter.5.cloned.1.call-start = ((), (), s32[]{:S(2)}) async-start(), calls=%async_computation.7 | async-start | bytes 327680 | tf_op jit(solution)/shard_map/reduce_scatter | solution.py:52
  125.0 6.1 %copy-start.6 = (bf16[8,32,1024]{2,1,0:T(8,128)(2,1)S(1)}, bf16[8,32,1024]{2,1,0:T(8,128)(2,1)}, u32[]{:S(2)}) copy-start(bf16[8,32,1024]{2,1,0:T(8,128)(2,1)} %copy-done.4) | copy-start | bytes 1572868
  125.0 6.1 %copy-start.10 = (bf16[256,1024]{1,0:T(8,128)(2,1)S(1)}, bf16[256,1024]{1,0:T(8,128)(2,1)}, u32[]{:S(2)}) copy-start(bf16[256,1024]{1,0:T(8,128)(2,1)} %copy-done.9) | copy-start | bytes 1572868
  131.1 2.1 copy-start.15
  133.2 3.3 %copy-start.1 = (f32[256,1024]{1,0:T(8,128)S(1)}, f32[256,1024]{1,0:T(8,128)}, u32[]{:S(2)}) copy-start(f32[256,1024]{1,0:T(8,128)} %gather_fusion) | copy-start | bytes 3145732
  133.2 3.3 %copy-start.3 = (f32[256,1024]{1,0:T(8,128)S(1)}, f32[256,1024]{1,0:T(8,128)}, u32[]{:S(2)}) copy-start(f32[256,1024]{1,0:T(8,128)} %copy-done.2) | copy-start | bytes 3145732
  133.2 24.9 %copy-start.61 = (f32[128]{0:T(128)S(1)}, f32[128]{0:T(128)}, u32[]{:S(2)}) copy-start(f32[128]{0:T(128)} %copy-done.60) | copy-start | bytes 1540
  133.2 43.1 %copy-start.65 = (f32[128]{0:T(128)S(1)}, f32[128]{0:T(128)}, u32[]{:S(2)}) copy-start(f32[128]{0:T(128)} %copy-done.64) | copy-start | bytes 1540
  176.4 29.1 %copy-start.19 = (f32[256,1]{0,1:T(1,128)S(1)}, f32[256,1]{0,1:T(1,128)}, u32[]{:S(2)}) copy-start(f32[256,1]{0,1:T(1,128)} %copy-done.18) | copy-start | bytes 3076
  176.4 29.1 %copy-start.21 = (f32[256,1]{0,1:T(1,128)S(1)}, f32[256,1]{0,1:T(1,128)}, u32[]{:S(2)}) copy-start(f32[256,1]{0,1:T(1,128)} %copy-done.20) | copy-start | bytes 3076
  176.4 29.1 %copy-start.23 = (f32[256,1]{0,1:T(1,128)S(1)}, f32[256,1]{0,1:T(1,128)}, u32[]{:S(2)}) copy-start(f32[256,1]{0,1:T(1,128)} %copy-done.22) | copy-start | bytes 3076
  176.4 29.1 %copy-start.25 = (f32[256,1]{0,1:T(1,128)S(1)}, f32[256,1]{0,1:T(1,128)}, u32[]{:S(2)}) copy-start(f32[256,1]{0,1:T(1,128)} %copy-done.24) | copy-start | bytes 3076
  176.4 29.1 %copy-start.27 = (f32[256,1]{0,1:T(1,128)S(1)}, f32[256,1]{0,1:T(1,128)}, u32[]{:S(2)}) copy-start(f32[256,1]{0,1:T(1,128)} %copy-done.26) | copy-start | bytes 3076
  176.4 29.1 %copy-start.29 = (f32[256,1]{0,1:T(1,128)S(1)}, f32[256,1]{0,1:T(1,128)}, u32[]{:S(2)}) copy-start(f32[256,1]{0,1:T(1,128)} %copy-done.28) | copy-start | bytes 3076
  176.4 29.1 %copy-start.31 = (f32[256,1]{0,1:T(1,128)S(1)}, f32[256,1]{0,1:T(1,128)}, u32[]{:S(2)}) copy-start(f32[256,1]{0,1:T(1,128)} %copy-done.30) | copy-start | bytes 3076
  176.4 29.1 %copy-start.33 = (f32[256,1]{0,1:T(1,128)S(1)}, f32[256,1]{0,1:T(1,128)}, u32[]{:S(2)}) copy-start(f32[256,1]{0,1:T(1,128)} %copy-done.32) | copy-start | bytes 3076
  176.4 29.1 %copy-start.35 = (f32[256,1]{0,1:T(1,128)S(1)}, f32[256,1]{0,1:T(1,128)}, u32[]{:S(2)}) copy-start(f32[256,1]{0,1:T(1,128)} %copy-done.34) | copy-start | bytes 3076
  176.5 29.1 %copy-start.37 = (f32[256,1]{0,1:T(1,128)S(1)}, f32[256,1]{0,1:T(1,128)}, u32[]{:S(2)}) copy-start(f32[256,1]{0,1:T(1,128)} %copy-done.36) | copy-start | bytes 3076
  176.5 29.1 %copy-start.39 = (f32[256,1]{0,1:T(1,128)S(1)}, f32[256,1]{0,1:T(1,128)}, u32[]{:S(2)}) copy-start(f32[256,1]{0,1:T(1,128)} %copy-done.38) | copy-start | bytes 3076
  176.5 29.1 %copy-start.41 = (f32[256,1]{0,1:T(1,128)S(1)}, f32[256,1]{0,1:T(1,128)}, u32[]{:S(2)}) copy-start(f32[256,1]{0,1:T(1,128)} %copy-done.40) | copy-start | bytes 3076
  176.5 29.1 %copy-start.43 = (f32[256,1]{0,1:T(1,128)S(1)}, f32[256,1]{0,1:T(1,128)}, u32[]{:S(2)}) copy-start(f32[256,1]{0,1:T(1,128)} %copy-done.42) | copy-start | bytes 3076
  176.5 29.1 %copy-start.45 = (f32[256,1]{0,1:T(1,128)S(1)}, f32[256,1]{0,1:T(1,128)}, u32[]{:S(2)}) copy-start(f32[256,1]{0,1:T(1,128)} %copy-done.44) | copy-start | bytes 3076
  176.5 29.1 %copy-start.47 = (f32[256,1]{0,1:T(1,128)S(1)}, f32[256,1]{0,1:T(1,128)}, u32[]{:S(2)}) copy-start(f32[256,1]{0,1:T(1,128)} %copy-done.46) | copy-start | bytes 3076
  176.5 29.1 %copy-start.49 = (f32[256,1]{0,1:T(1,128)S(1)}, f32[256,1]{0,1:T(1,128)}, u32[]{:S(2)}) copy-start(f32[256,1]{0,1:T(1,128)} %copy-done.48) | copy-start | bytes 3076
  176.5 29.1 %copy-start.51 = (f32[256,1]{0,1:T(1,128)S(1)}, f32[256,1]{0,1:T(1,128)}, u32[]{:S(2)}) copy-start(f32[256,1]{0,1:T(1,128)} %copy-done.50) | copy-start | bytes 3076
  176.5 29.1 %copy-start.53 = (f32[256,1]{0,1:T(1,128)S(1)}, f32[256,1]{0,1:T(1,128)}, u32[]{:S(2)}) copy-start(f32[256,1]{0,1:T(1,128)} %copy-done.52) | copy-start | bytes 3076
  176.5 29.1 %copy-start.55 = (f32[256,1]{0,1:T(1,128)S(1)}, f32[256,1]{0,1:T(1,128)}, u32[]{:S(2)}) copy-start(f32[256,1]{0,1:T(1,128)} %copy-done.54) | copy-start | bytes 3076
  176.6 29.1 %copy-start.57 = (f32[256,1]{0,1:T(1,128)S(1)}, f32[256,1]{0,1:T(1,128)}, u32[]{:S(2)}) copy-start(f32[256,1]{0,1:T(1,128)} %copy-done.56) | copy-start | bytes 3076
  176.6 29.1 %copy-start.59 = (f32[256,1]{0,1:T(1,128)S(1)}, f32[256,1]{0,1:T(1,128)}, u32[]{:S(2)}) copy-start(f32[256,1]{0,1:T(1,128)} %copy-done.58) | copy-start | bytes 3076
  178.0 27.5 %collective-permute-start.2 = (bf16[256,15]{0,1:T(8,128)(2,1)S(1)}, bf16[256,15]{0,1:T(8,128)(2,1)S(1)}, u32[]{:S(2)}, u32[]{:S(2)}) collective-permute-start(bf16[256,15]{0,1:T(8,128)(2,1)S(1)} %get-tuple-element.68), channel_id=1, source_target_pairs={{0,4},{4,8},{8,12},{12,16},{16,20},{20,24},{24,28},{28,0},{1,5},{5... | collective-permute-start | bytes 23048 | tf_op jit(solution)/shard_map/ppermute | solution.py:16
  178.1 27.4 %collective-permute-start.3 = (bf16[256,15]{0,1:T(8,128)(2,1)S(1)}, bf16[256,15]{0,1:T(8,128)(2,1)S(1)}, u32[]{:S(2)}, u32[]{:S(2)}) collective-permute-start(bf16[256,15]{0,1:T(8,128)(2,1)S(1)} %get-tuple-element.69), channel_id=1, source_target_pairs={{4,0},{8,4},{12,8},{16,12},{20,16},{24,20},{28,24},{0,28},{5,1},{9... | collective-permute-start | bytes 23048 | tf_op jit(solution)/shard_map/ppermute | solution.py:18
  (12 other events, 13.8 us)
Sparse Core Ops, SparseCore 0:
  119.7 18.0 reduce-scatter.2
  140.1 17.9 reduce-scatter.4
where the time goes:
time: 215 us; the launch traced here: 214 us
  blocking collectives  81.2 us (38%)
  waiting for transfers between devices  32.6 us (15%)
  local copies, waits for them, and re-layouts  24.1 us (11%)
  starting transfers between devices  22.3 us (10%)
  matrix products  20.8 us (10%)
  other arithmetic  17.6 us (8%)
  between operations  15.1 us (7%)
    psum x1, blocking collectives, local(): grad_taps, grad_gain = lax.psum((tap_local, gain_local), 'ctx')  23.3 us
    reduce_scatter x2, waiting for transfers between devices, bring_back(): lax.psum_scatter(term.astype(jnp.bfloat16), 'exp', scatter_dimension=1, t...  21.3 us
    psum x1, blocking collectives, local(): lax.psum(jnp.sum(d_normed * gain_f[:, None] * mixed_f, axis=0), 'exp')  17.2 us
    all_gather x1, blocking collectives, local(): lax.all_gather(grad_out, 'exp', axis=0, tiled=True)  15 us
    all_gather x1, blocking collectives, local(): lax.all_gather(normed_part, 'exp', axis=0, tiled=True)  13.8 us
    psum x1, blocking collectives, local(): squares = lax.psum(jnp.sum(mixed_f * mixed_f, axis=0), 'exp')  11.9 us
    all_to_all x2, starting transfers between devices, bring_back(): lax.all_to_all(values.reshape(experts, capacity, width).astype(jnp.bfloat...  7.65 us
    gather x3, local copies, waits for them, and re-layouts, bring_back(): picked = back.reshape(experts * capacity, width)[dest]  7 us
  transfers between devices with their start and end apart: 10, of which 4 were waited for; matrix products, arithmetic and copies ran while one was open for 23% of the time, Pallas kernels for 0%

commit v1 on v0

--- a/solution.py
+++ b/solution.py
@@ -4,6 +4,22 @@
 from jax.sharding import PartitionSpec as P
 
 EPS = 1e-05
+
+
+def pairwise_exchange(x, axis, split, join):
+    ways, here = (lax.axis_size(axis), lax.axis_index(axis))
+    width = x.shape[split] // ways
+    shape = list(x.shape)
+    shape[split] = width
+    height = shape[join]
+    shape[join] = height * ways
+    full = jnp.zeros(shape, x.dtype)
+    for mask in range(ways):
+        part = lax.dynamic_slice_in_dim(x, (here ^ mask) * width, width, axis=split)
+        if mask:
+            part = lax.ppermute(part, axis, [(d, d ^ mask) for d in range(ways)])
+        full = lax.dynamic_update_slice_in_dim(full, part, (here ^ mask) * height, axis=join)
+    return full
 
 
 def padded_2(cells, sides, width):
@@ -87,7 +103,7 @@
     send_x = empty.at[dest].set(token_rows).reshape(experts, capacity, width)
     send_dy = empty.at[dest].set(scaled_rows).reshape(experts, capacity, width)
     recv_x, recv_dy = (
-        lax.all_to_all(send_x, "ctx", split_axis=0, concat_axis=0, tiled=True),
+        pairwise_exchange(send_x, "ctx", 0, 0),
         lax.all_to_all(send_dy, "ctx", split_axis=0, concat_axis=0, tiled=True),
     )
     rows_x = recv_x.reshape(-1, width)

time: 215 us -> 216 us (level)
  starting transfers between devices: 22.3 us -> 25.4 us
    ppermute x0 -> x7, starting transfers between devices: none -> 7.2 us  [pairwise_exchange(): part = lax.ppermute(part, axis, [(d, d ^ mask) for d in range(ways)])]
    ppermute x0 -> x7, waiting for transfers between devices: none -> 6.39 us  [pairwise_exchange(): part = lax.ppermute(part, axis, [(d, d ^ mask) for d in range(ways)])]
    all_to_all x1 -> x0, waiting for transfers between devices: 5.58 us -> none  [local(): lax.all_to_all(send_x, 'ctx', split_axis=0, concat_axis=0, tiled=True)]
    all_to_all x1 -> x0, starting transfers between devices: 4.09 us -> none  [local(): lax.all_to_all(send_x, 'ctx', split_axis=0, concat_axis=0, tiled=True)]
  transfers between devices with their start and end apart: 10 -> 16, of which waited for: 4 -> 5; matrix products, arithmetic and copies ran while one was open for 23% -> 22% of each run, Pallas kernels for 0% -> 0%
where the time goes in v1:
time: 216 us; the launch traced here: 215 us
  blocking collectives  81.1 us (38%)
  waiting for transfers between devices  33.6 us (16%)
  starting transfers between devices  25.4 us (12%)
  local copies, waits for them, and re-layouts  24.3 us (11%)
  matrix products  19.1 us (9%)
  other arithmetic  16.4 us (8%)
  between operations  15.3 us (7%)
    psum x1, blocking collectives, local(): grad_taps, grad_gain = lax.psum((tap_local, gain_local), 'ctx')  23.3 us
    reduce_scatter x2, waiting for transfers between devices, bring_back(): lax.psum_scatter(term.astype(jnp.bfloat16), 'exp', scatter_dimension=1, t...  21.4 us
    psum x1, blocking collectives, local(): lax.psum(jnp.sum(d_normed * gain_f[:, None] * mixed_f, axis=0), 'exp')  17.2 us
    all_gather x1, blocking collectives, local(): lax.all_gather(grad_out, 'exp', axis=0, tiled=True)  15 us
    all_gather x1, blocking collectives, local(): lax.all_gather(normed_part, 'exp', axis=0, tiled=True)  13.8 us
    psum x1, blocking collectives, local(): squares = lax.psum(jnp.sum(mixed_f * mixed_f, axis=0), 'exp')  11.8 us
    all_to_all x2, starting transfers between devices, bring_back(): lax.all_to_all(values.reshape(experts, capacity, width).astype(jnp.bfloat...  7.83 us
    ppermute x7, starting transfers between devices, pairwise_exchange(): part = lax.ppermute(part, axis, [(d, d ^ mask) for d in range(ways)])  7.2 us
  transfers between devices with their start and end apart: 16, of which 5 were waited for; matrix products, arithmetic and copies ran while one was open for 22% of the time, Pallas kernels for 0%

profile of v1, /device:TPU:0, one launch (start us, length us, event | category | flops | bytes accessed | tf_op | source)
XLA Modules:
  0.0 215.2 jit_solution(8067262728108988700)
XLA Ops:
  7.2 1.1 copy.28
  8.3 0.5 collective-permute-start
  8.8 2.9 %collective-permute-start.1 = (bf16[256,15]{0,1:T(8,128)(2,1)S(1)}, bf16[256,15]{0,1:T(8,128)(2,1)S(1)}, u32[]{:S(2)}, u32[]{:S(2)}) collective-permute-start(bf16[256,15]{0,1:T(8,128)(2,1)S(1)} %get-tuple-element.80), channel_id=1, source_target_pairs={{4,0},{8,4},{12,8},{16,12},{20,16},{24,20},{28,24},{0,28},{5,1},{9... | collective-permute-start | bytes 23048 | tf_op jit(solution)/shard_map/ppermute | solution.py:34
  11.7 0.7 broadcast_multiply_fusion
  12.4 0.8 copy.33
  13.3 0.1 eq.25
  13.6 0.1 mul.817
  13.7 0.8 copy.35
  14.7 0.6 reduce-window.6
  15.3 0.2 slice_reduce_fusion
  15.5 15.0 %all_gather.7 = bf16[1024,128]{1,0:T(8,128)(2,1)S(1)} all-gather(bf16[256,128]{1,0:T(8,128)(2,1)} %param.17), channel_id=1, replica_groups=mesh['ctx'=8,'exp'=4] {'exp'}, dimensions={0}, use_global_device_ids=true | all-gather | bytes 327680 | tf_op jit(solution)/shard_map/all_gather | solution.py:95
  30.6 0.2 copy.37
  30.8 1.3 broadcast_in_dim.17
  32.1 1.9 convert_element_type.108
  34.2 2.5 %scatter_custom_fusion.1 = bf16[256,1024]{1,0:T(8,128)(2,1)} fusion(s32[256]{0:T(256)S(1)} %bitcast.246, f32[256,1024]{1,0:T(8,128)S(1)} %convert_element_type.108, f32[256]{0:T(256)S(1)} %mul.828, bf16[]{:T(256)} %constant.18.clone.1), kind=kCustom, calls=%fused_computation.29 | custom fusion | flops 524288 | bytes 1573890 | tf_op jit(solution)/shard_map/scatter | solution.py:104
  36.7 4.1 %all-to-all-start.1 = ((bf16[8,32,1024]{2,1,0:T(8,128)(2,1)}), bf16[8,32,1024]{2,1,0:T(8,128)(2,1)}, u32[]{:S(2)}, u32[]{:S(2)}) async-start(bf16[8,32,1024]{2,1,0:T(8,128)(2,1)} %bitcast.149), calls=%async_computation.2 | async-start | bytes 1048576 | tf_op jit(solution)/shard_map/all_to_all | solution.py:107
  41.3 0.5 fusion.28
  41.9 11.8 %psum.35 = f32[128]{0:T(128)S(1)} all-reduce(f32[128]{0:T(128)S(1)} %get-tuple-element.62), channel_id=1, replica_groups=mesh['ctx'=8,'exp'=4] {'exp'}, use_global_device_ids=true, to_apply=%region_4.5 | all-reduce | flops 128 | bytes 1024 | tf_op jit(solution)/shard_map/psum | solution.py:90
  53.8 13.8 %all_gather.6 = bf16[1024,128]{0,1:T(8,128)(2,1)S(1)} all-gather(bf16[256,128]{0,1:T(8,128)(2,1)S(1)} %fusion.27), channel_id=1, replica_groups=mesh['ctx'=8,'exp'=4] {'exp'}, dimensions={0}, use_global_device_ids=true | all-gather | bytes 327680 | tf_op jit(solution)/shard_map/all_gather | solution.py:94
  67.6 0.3 broadcast_in_dim.16
  67.9 1.0 reshape.158
  68.9 2.3 %scatter_custom_fusion = bf16[256,1024]{1,0:T(8,128)(2,1)S(1)} fusion(s32[256]{0:T(256)S(1)} %bitcast.247, bf16[256,1024]{1,0:T(8,128)(2,1)} %reshape.158, bf16[]{:T(256)} %constant.18.clone.1), kind=kCustom, calls=%fused_computation.41 | custom fusion | bytes 524800 | tf_op jit(solution)/shard_map/scatter | solution.py:103
  71.4 2.9 %collective-permute-start.8 = (bf16[1,32,1024]{2,1,0:T(8,128)(2,1)S(1)}, bf16[1,32,1024]{2,1,0:T(8,128)(2,1)S(1)}, u32[]{:S(2)}, u32[]{:S(2)}) collective-permute-start(bf16[1,32,1024]{2,1,0:T(8,128)(2,1)S(1)} %get-tuple-element.67), channel_id=1, source_target_pairs={{0,28},{4,24},{8,20},{12,16},{16,12},{20,8},{24,4},{28,0},{1,29},{... | collective-permute-start | bytes 196616 | tf_op jit(solution)/shard_map/ppermute | solution.py:20
  74.5 1.3 collective-permute-start.6
  75.8 0.6 collective-permute-start.5
  76.4 1.5 collective-permute-start.3
  77.9 2.8 %collective-permute-done.3 = bf16[1,32,1024]{2,1,0:T(8,128)(2,1)S(1)} collective-permute-done((bf16[1,32,1024]{2,1,0:T(8,128)(2,1)S(1)}, bf16[1,32,1024]{2,1,0:T(8,128)(2,1)S(1)}, u32[]{:S(2)}, u32[]{:S(2)}) %collective-permute-start.3) | collective-permute-done | bytes 65568 | tf_op jit(solution)/shard_map/ppermute | solution.py:20
  80.7 0.7 collective-permute-start.4
  81.4 3.6 %collective-permute-done.4 = bf16[1,32,1024]{2,1,0:T(8,128)(2,1)S(1)} collective-permute-done((bf16[1,32,1024]{2,1,0:T(8,128)(2,1)S(1)}, bf16[1,32,1024]{2,1,0:T(8,128)(2,1)S(1)}, u32[]{:S(2)}, u32[]{:S(2)}) %collective-permute-start.4) | collective-permute-done | bytes 65568 | tf_op jit(solution)/shard_map/ppermute | solution.py:20
  85.1 1.7 fusion.6
  86.8 2.6 %fusion.2 = f32[256,1024]{1,0:T(8,128)S(1)} fusion(bf16[256,1024]{1,0:T(8,128)(2,1)} %bitcast.47, bf16[1,1024,1024]{2,1,0:T(8,128)(2,1)} %param.16), kind=kOutput, calls=%fused_computation.6 | convolution fusion | flops 536870912 | bytes 3670016 | tf_op jit(solution)/shard_map/dot_general | solution.py:124
  89.4 2.0 multiply_convert_fusion.1
  91.4 0.8 copy-done.15
  92.2 1.5 fusion.15
  93.7 3.7 %all-to-all-start = ((bf16[8,32,1024]{2,1,0:T(8,128)(2,1)}), bf16[8,32,1024]{2,1,0:T(8,128)(2,1)S(1)}, u32[]{:S(2)}, u32[]{:S(2)}) async-start(bf16[8,32,1024]{2,1,0:T(8,128)(2,1)} %fusion.15), calls=%async_computation | async-start | bytes 1048576 | tf_op jit(solution)/shard_map/all_to_all | solution.py:59
  97.4 2.4 %fusion.4 = f32[256,1024]{1,0:T(8,128)S(1)} fusion(bf16[256,1024]{1,0:T(8,128)(2,1)S(1)} %get-tuple-element.66, bf16[1,1024,1024]{2,1,0:T(8,128)(2,1)} %param.15), kind=kOutput, calls=%fused_computation.8 | convolution fusion | flops 536870912 | bytes 3670016 | tf_op jit(solution)/shard_map/dot_general | solution.py:139
  99.8 1.6 fusion.18
  101.4 5.7 %all-to-all-done = bf16[8,32,1024]{2,1,0:T(8,128)(2,1)S(1)} async-done(((bf16[8,32,1024]{2,1,0:T(8,128)(2,1)}), bf16[8,32,1024]{2,1,0:T(8,128)(2,1)S(1)}, u32[]{:S(2)}, u32[]{:S(2)}) %all-to-all-start) | async-done | bytes 524320 | tf_op jit(solution)/shard_map/all_to_all | solution.py:59
  107.2 4.2 %all-to-all-start.2 = ((bf16[8,32,1024]{2,1,0:T(8,128)(2,1)}), bf16[8,32,1024]{2,1,0:T(8,128)(2,1)}, u32[]{:S(2)}, u32[]{:S(2)}) async-start(bf16[8,32,1024]{2,1,0:T(8,128)(2,1)} %bitcast.48), calls=%async_computation.3 | async-start | bytes 1048576 | tf_op jit(solution)/shard_map/all_to_all | solution.py:59
  111.4 1.1 bitcast_convert_fusion.1
  112.5 2.1 gather_fusion
  114.6 2.9 %gather.9 = f32[128,2,1024]{2,1,0:T(2,128)} reshape(f32[256,1024]{1,0:T(8,128)} %gather_fusion) | data formatting | bytes 2097152 | tf_op jit(solution)/shard_map/gather | solution.py:66
  117.5 3.3 %multiply_reduce_fusion.1 = bf16[128,1024]{1,0:T(8,128)(2,1)} fusion(f32[128,2,1024]{2,1,0:T(2,128)} %gather.9, f32[128,2]{1,0:T(8,128)S(1)} %copy.35), kind=kLoop, calls=%fused_computation.26 | loop fusion | flops 393216 | bytes 1311744 | tf_op jit(solution)/shard_map/reduce_sum | solution.py:67
  121.1 2.1 convert_bitcast_fusion.2
  123.2 1.1 bitcast_convert_fusion
  124.3 2.0 gather_fusion.1
  126.3 2.9 %reshape.132 = f32[128,2,1024]{2,1,0:T(2,128)} reshape(f32[256,1024]{1,0:T(8,128)} %gather_fusion.1) | data formatting | bytes 2097152 | tf_op jit(solution)/shard_map/reshape | solution.py:67
  129.2 3.2 %reduce_sum.348 = bf16[128,1024]{1,0:T(8,128)(2,1)} reduce(f32[128,2,1024]{2,1,0:T(2,128)} %reshape.132, f32[]{:T(128)} %constant.8.clone.1), dimensions={1}, to_apply=%region_9.10 | reduce | flops 131072 | bytes 1310724 | tf_op jit(solution)/shard_map/reduce_sum | solution.py:67
  132.5 2.1 convert_bitcast_fusion.1
  134.6 3.3 %convert_bitcast_fusion = bf16[1,1024,1024]{2,1,0:T(8,128)(2,1)} fusion(bf16[256,1024]{1,0:T(8,128)(2,1)S(1)} %copy-done.16, bf16[256,1024]{1,0:T(8,128)(2,1)} %bitcast.47), kind=kOutput, calls=%fused_computation.16 | convolution fusion | flops 537919488 | bytes 3145728 | tf_op jit(solution)/shard_map/dot_general | solution.py:127
  137.8 0.2 multiply_reduce_fusion
  138.0 0.1 reshape.133
  138.2 1.2 reduce-scatter.3.cloned.1.call-done
  139.3 20.2 %reduce-scatter.5.cloned.1.call-done = bf16[128,256]{1,0:T(8,128)(2,1)} async-done(((bf16[128,1024]{1,0:T(8,128)(2,1)}), bf16[128,256]{1,0:T(8,128)(2,1)}) %reduce-scatter.5.cloned.1.call-update) | async-done | bytes 65552 | tf_op jit(solution)/shard_map/reduce_scatter | solution.py:68
  159.6 1.0 fusion.33
  160.6 17.2 %all-reduce.1 = (f32[128]{0:T(128)S(1)}, f32[128,2]{1,0:T(8,128)S(1)}) all-reduce(f32[128]{0:T(128)S(1)} %get-tuple-element.56, f32[128,2]{1,0:T(8,128)S(1)} %reshape.133), channel_id=1, replica_groups=mesh['ctx'=8,'exp'=4] {'exp'}, use_global_device_ids=true, to_apply=%region_12.13 | all-reduce | flops 384 | bytes 3072 | tf_op jit(solution)/shard_map/psum | solution.py:145
  178.0 1.2 multiply_reduce_fusion.2
  179.2 0.2 multiply_reduce_fusion.20
  179.5 2.6 %collective-permute-start.10 = (bf16[256,15]{0,1:T(8,128)(2,1)S(1)}, bf16[256,15]{0,1:T(8,128)(2,1)S(1)}, u32[]{:S(2)}, u32[]{:S(2)}) collective-permute-start(bf16[256,15]{0,1:T(8,128)(2,1)S(1)} %get-tuple-element.77), channel_id=1, source_target_pairs={{4,0},{8,4},{12,8},{16,12},{20,16},{24,20},{28,24},{0,28},{5,1},{9... | collective-permute-start | bytes 23048 | tf_op jit(solution)/shard_map/ppermute | solution.py:34
  182.3 23.3 %all-reduce = (f32[256,31]{0,1:T(8,128)}, f32[256]{0:T(256)}) all-reduce(f32[256,31]{0,1:T(8,128)S(1)} %stack.127, f32[256]{0:T(256)S(1)} %get-tuple-element.55), channel_id=1, replica_groups=mesh['ctx'=8,'exp'=4] {'ctx'}, use_global_device_ids=true, to_apply=%region_44.45 | all-reduce | flops 8192 | bytes 65536 | tf_op jit(solution)/shard_map/psum | solution.py:163
  205.5 0.6 copy.41
  206.2 0.7 copy.39
  207.2 0.4 fusion.35
  207.6 0.7 copy.40
  (180 shorter events, 1.8 us)
Async XLA Ops:
  7.2 82.2 %copy-start = (bf16[1,1024,1024]{2,1,0:T(8,128)(2,1)S(1)}, bf16[1,1024,1024]{2,1,0:T(8,128)(2,1)}, u32[]{:S(2)}) copy-start(bf16[1,1024,1024]{2,1,0:T(8,128)(2,1)} %param.14) | copy-start | bytes 6291460
  8.3 32.9 %collective-permute-start = (bf16[256,15]{0,1:T(8,128)(2,1)S(1)}, bf16[256,15]{0,1:T(8,128)(2,1)S(1)}, u32[]{:S(2)}, u32[]{:S(2)}) collective-permute-start(bf16[256,15]{0,1:T(8,128)(2,1)S(1)} %get-tuple-element.79), channel_id=1, source_target_pairs={{0,4},{4,8},{8,12},{12,16},{16,20},{20,24},{24,28},{28,0},{1,5},{5... | collective-permute-start | bytes 23048 | tf_op jit(solution)/shard_map/ppermute | solution.py:32
  8.8 32.4 %collective-permute-start.1 = (bf16[256,15]{0,1:T(8,128)(2,1)S(1)}, bf16[256,15]{0,1:T(8,128)(2,1)S(1)}, u32[]{:S(2)}, u32[]{:S(2)}) collective-permute-start(bf16[256,15]{0,1:T(8,128)(2,1)S(1)} %get-tuple-element.80), channel_id=1, source_target_pairs={{4,0},{8,4},{12,8},{16,12},{20,16},{24,20},{28,24},{0,28},{5,1},{9... | collective-permute-start | bytes 23048 | tf_op jit(solution)/shard_map/ppermute | solution.py:34
  32.1 8.7 %copy-start.18 = (f32[256,31]{0,1:T(8,128)S(1)}, f32[256,31]{0,1:T(8,128)}, u32[]{:S(2)}) copy-start(f32[256,31]{0,1:T(8,128)} %param.10) | copy-start | bytes 95236
  32.1 9.0 %copy-start.63 = (bf16[256]{0:T(256)(128)(2,1)S(1)}, bf16[256]{0:T(256)(128)(2,1)}, u32[]{:S(2)}) copy-start(bf16[256]{0:T(256)(128)(2,1)} %param.11) | copy-start | bytes 1540
  34.1 7.2 %copy-start.2 = (f32[256,1024]{1,0:T(8,128)}, f32[256,1024]{1,0:T(8,128)S(1)}, u32[]{:S(2)}) copy-start(f32[256,1024]{1,0:T(8,128)S(1)} %convert_element_type.108) | copy-start | bytes 3145732
  36.7 50.1 %all-to-all-start.1 = ((bf16[8,32,1024]{2,1,0:T(8,128)(2,1)}), bf16[8,32,1024]{2,1,0:T(8,128)(2,1)}, u32[]{:S(2)}, u32[]{:S(2)}) async-start(bf16[8,32,1024]{2,1,0:T(8,128)(2,1)} %bitcast.149), calls=%async_computation.2 | async-start | bytes 1048576 | tf_op jit(solution)/shard_map/all_to_all | solution.py:107
  40.9 0.9 copy-start.19
  40.9 0.8 copy-start.21
  40.9 0.8 copy-start.23
  40.9 0.8 copy-start.25
  53.7 17.6 %copy-start.64 = (f32[128]{0:T(128)}, f32[128]{0:T(128)S(1)}, u32[]{:S(2)}) copy-start(f32[128]{0:T(128)S(1)} %psum.35) | copy-start | bytes 1540
  53.7 17.6 %copy-start.61 = (f32[128]{0:T(128)}, f32[128]{0:T(128)S(1)}, u32[]{:S(2)}) copy-start(f32[128]{0:T(128)S(1)} %add_rsqrt_fusion) | copy-start | bytes 1540
  71.2 13.9 %copy-start.4 = (bf16[1,1024,1024]{2,1,0:T(8,128)(2,1)S(1)}, bf16[1,1024,1024]{2,1,0:T(8,128)(2,1)}, u32[]{:S(2)}) copy-start(bf16[1,1024,1024]{2,1,0:T(8,128)(2,1)} %param.15) | copy-start | bytes 6291460
  71.3 5.1 %collective-permute-start.2 = (bf16[1,32,1024]{2,1,0:T(8,128)(2,1)S(1)}, bf16[1,32,1024]{2,1,0:T(8,128)(2,1)S(1)}, u32[]{:S(2)}, u32[]{:S(2)}) collective-permute-start(bf16[1,32,1024]{2,1,0:T(8,128)(2,1)S(1)} %get-tuple-element.73), channel_id=1, source_target_pairs={{0,4},{4,0},{8,12},{12,8},{16,20},{20,16},{24,28},{28,24},{1,5},{5... | collective-permute-start | bytes 196616 | tf_op jit(solution)/shard_map/ppermute | solution.py:20
  71.4 13.6 %collective-permute-start.8 = (bf16[1,32,1024]{2,1,0:T(8,128)(2,1)S(1)}, bf16[1,32,1024]{2,1,0:T(8,128)(2,1)S(1)}, u32[]{:S(2)}, u32[]{:S(2)}) collective-permute-start(bf16[1,32,1024]{2,1,0:T(8,128)(2,1)S(1)} %get-tuple-element.67), channel_id=1, source_target_pairs={{0,28},{4,24},{8,20},{12,16},{16,12},{20,8},{24,4},{28,0},{1,29},{... | collective-permute-start | bytes 196616 | tf_op jit(solution)/shard_map/ppermute | solution.py:20
  74.4 10.7 %collective-permute-start.7 = (bf16[1,32,1024]{2,1,0:T(8,128)(2,1)S(1)}, bf16[1,32,1024]{2,1,0:T(8,128)(2,1)S(1)}, u32[]{:S(2)}, u32[]{:S(2)}) collective-permute-start(bf16[1,32,1024]{2,1,0:T(8,128)(2,1)S(1)} %get-tuple-element.68), channel_id=1, source_target_pairs={{0,24},{4,28},{8,16},{12,20},{16,8},{20,12},{24,0},{28,4},{1,25},{... | collective-permute-start | bytes 196616 | tf_op jit(solution)/shard_map/ppermute | solution.py:20
  74.5 10.5 %collective-permute-start.6 = (bf16[1,32,1024]{2,1,0:T(8,128)(2,1)S(1)}, bf16[1,32,1024]{2,1,0:T(8,128)(2,1)S(1)}, u32[]{:S(2)}, u32[]{:S(2)}) collective-permute-start(bf16[1,32,1024]{2,1,0:T(8,128)(2,1)S(1)} %get-tuple-element.69), channel_id=1, source_target_pairs={{0,20},{4,16},{8,28},{12,24},{16,4},{20,0},{24,12},{28,8},{1,21},{... | collective-permute-start | bytes 196616 | tf_op jit(solution)/shard_map/ppermute | solution.py:20
  75.8 9.2 %collective-permute-start.5 = (bf16[1,32,1024]{2,1,0:T(8,128)(2,1)S(1)}, bf16[1,32,1024]{2,1,0:T(8,128)(2,1)S(1)}, u32[]{:S(2)}, u32[]{:S(2)}) collective-permute-start(bf16[1,32,1024]{2,1,0:T(8,128)(2,1)S(1)} %get-tuple-element.70), channel_id=1, source_target_pairs={{0,16},{4,20},{8,24},{12,28},{16,0},{20,4},{24,8},{28,12},{1,17},{... | collective-permute-start | bytes 196616 | tf_op jit(solution)/shard_map/ppermute | solution.py:20
  76.4 4.3 %collective-permute-start.3 = (bf16[1,32,1024]{2,1,0:T(8,128)(2,1)S(1)}, bf16[1,32,1024]{2,1,0:T(8,128)(2,1)S(1)}, u32[]{:S(2)}, u32[]{:S(2)}) collective-permute-start(bf16[1,32,1024]{2,1,0:T(8,128)(2,1)S(1)} %get-tuple-element.72), channel_id=1, source_target_pairs={{0,8},{4,12},{8,0},{12,4},{16,24},{20,28},{24,16},{28,20},{1,9},{5... | collective-permute-start | bytes 196616 | tf_op jit(solution)/shard_map/ppermute | solution.py:20
  80.7 4.3 %collective-permute-start.4 = (bf16[1,32,1024]{2,1,0:T(8,128)(2,1)S(1)}, bf16[1,32,1024]{2,1,0:T(8,128)(2,1)S(1)}, u32[]{:S(2)}, u32[]{:S(2)}) collective-permute-start(bf16[1,32,1024]{2,1,0:T(8,128)(2,1)S(1)} %get-tuple-element.71), channel_id=1, source_target_pairs={{0,12},{4,8},{8,4},{12,0},{16,28},{20,24},{24,20},{28,16},{1,13},{... | collective-permute-start | bytes 196616 | tf_op jit(solution)/shard_map/ppermute | solution.py:20
  85.1 4.3 %copy-start.5 = (bf16[8,32,1024]{2,1,0:T(8,128)(2,1)}, bf16[8,32,1024]{2,1,0:T(8,128)(2,1)S(1)}, u32[]{:S(2)}) copy-start(bf16[8,32,1024]{2,1,0:T(8,128)(2,1)S(1)} %constant_dynamic-update-slice_fusion.6) | copy-start | bytes 1572868
  86.8 2.6 %copy-start.14 = (f32[256,1024]{1,0:T(8,128)S(1)}, f32[256,1024]{1,0:T(8,128)}, u32[]{:S(2)}) copy-start(f32[256,1024]{1,0:T(8,128)} %fusion.6) | copy-start | bytes 3145732
  89.4 2.8 %copy-start.8 = (bf16[1,1024,1024]{2,1,0:T(8,128)(2,1)S(1)}, bf16[1,1024,1024]{2,1,0:T(8,128)(2,1)}, u32[]{:S(2)}) copy-start(bf16[1,1024,1024]{2,1,0:T(8,128)(2,1)} %param.16) | copy-start | bytes 6291460
  91.4 6.0 %copy-start.10 = (bf16[256,1024]{1,0:T(8,128)(2,1)}, bf16[256,1024]{1,0:T(8,128)(2,1)S(1)}, u32[]{:S(2)}) copy-start(bf16[256,1024]{1,0:T(8,128)(2,1)S(1)} %get-tuple-element.66) | copy-start | bytes 1572868
  93.7 13.4 %all-to-all-start = ((bf16[8,32,1024]{2,1,0:T(8,128)(2,1)}), bf16[8,32,1024]{2,1,0:T(8,128)(2,1)S(1)}, u32[]{:S(2)}, u32[]{:S(2)}) async-start(bf16[8,32,1024]{2,1,0:T(8,128)(2,1)} %fusion.15), calls=%async_computation | async-start | bytes 1048576 | tf_op jit(solution)/shard_map/all_to_all | solution.py:59
  97.4 2.4 %copy-start.12 = (bf16[256,1024]{1,0:T(8,128)(2,1)S(1)}, bf16[256,1024]{1,0:T(8,128)(2,1)}, u32[]{:S(2)}) copy-start(bf16[256,1024]{1,0:T(8,128)(2,1)} %get-tuple-element.64) | copy-start | bytes 1572868
  107.2 4.2 %copy-start.9 = (bf16[8,32,1024]{2,1,0:T(8,128)(2,1)}, bf16[8,32,1024]{2,1,0:T(8,128)(2,1)S(1)}, u32[]{:S(2)}) copy-start(bf16[8,32,1024]{2,1,0:T(8,128)(2,1)S(1)} %all-to-all-done) | copy-start | bytes 1572868
  107.2 16.0 %all-to-all-start.2 = ((bf16[8,32,1024]{2,1,0:T(8,128)(2,1)}), bf16[8,32,1024]{2,1,0:T(8,128)(2,1)}, u32[]{:S(2)}, u32[]{:S(2)}) async-start(bf16[8,32,1024]{2,1,0:T(8,128)(2,1)} %bitcast.48), calls=%async_computation.3 | async-start | bytes 1048576 | tf_op jit(solution)/shard_map/all_to_all | solution.py:59
  111.3 28.0 %reduce-scatter.3.cloned.1.call-start = ((), (), s32[]{:S(2)}) async-start(), calls=%async_computation.5 | async-start | bytes 327680 | tf_op jit(solution)/shard_map/reduce_scatter | solution.py:68
  114.6 6.3 %copy-start.17 = (bf16[256,128]{1,0:T(8,128)(2,1)S(1)}, bf16[256,128]{1,0:T(8,128)(2,1)}, u32[]{:S(2)}) copy-start(bf16[256,128]{1,0:T(8,128)(2,1)} %param.17) | copy-start | bytes 196612
  114.6 6.4 %copy-start.6 = (bf16[8,32,1024]{2,1,0:T(8,128)(2,1)S(1)}, bf16[8,32,1024]{2,1,0:T(8,128)(2,1)}, u32[]{:S(2)}) copy-start(bf16[8,32,1024]{2,1,0:T(8,128)(2,1)} %copy-done.5) | copy-start | bytes 1572868
  114.6 6.5 %copy-start.13 = (bf16[256,1024]{1,0:T(8,128)(2,1)S(1)}, bf16[256,1024]{1,0:T(8,128)(2,1)}, u32[]{:S(2)}) copy-start(bf16[256,1024]{1,0:T(8,128)(2,1)} %get-tuple-element.64) | copy-start | bytes 1572868
  120.9 38.7 %reduce-scatter.5.cloned.1.call-start = ((), (), s32[]{:S(2)}) async-start(), calls=%async_computation.6 | async-start | bytes 327680 | tf_op jit(solution)/shard_map/reduce_scatter | solution.py:68
  126.3 6.1 %copy-start.7 = (bf16[8,32,1024]{2,1,0:T(8,128)(2,1)S(1)}, bf16[8,32,1024]{2,1,0:T(8,128)(2,1)}, u32[]{:S(2)}) copy-start(bf16[8,32,1024]{2,1,0:T(8,128)(2,1)} %copy-done.5) | copy-start | bytes 1572868
  126.3 6.1 %copy-start.11 = (bf16[256,1024]{1,0:T(8,128)(2,1)S(1)}, bf16[256,1024]{1,0:T(8,128)(2,1)}, u32[]{:S(2)}) copy-start(bf16[256,1024]{1,0:T(8,128)(2,1)} %copy-done.10) | copy-start | bytes 1572868
  132.5 2.1 copy-start.16
  134.5 3.3 %copy-start.1 = (f32[256,1024]{1,0:T(8,128)S(1)}, f32[256,1024]{1,0:T(8,128)}, u32[]{:S(2)}) copy-start(f32[256,1024]{1,0:T(8,128)} %gather_fusion) | copy-start | bytes 3145732
  134.5 3.3 %copy-start.3 = (f32[256,1024]{1,0:T(8,128)S(1)}, f32[256,1024]{1,0:T(8,128)}, u32[]{:S(2)}) copy-start(f32[256,1024]{1,0:T(8,128)} %copy-done.2) | copy-start | bytes 3145732
  134.6 25.0 %copy-start.62 = (f32[128]{0:T(128)S(1)}, f32[128]{0:T(128)}, u32[]{:S(2)}) copy-start(f32[128]{0:T(128)} %copy-done.61) | copy-start | bytes 1540
  134.6 43.2 %copy-start.65 = (f32[128]{0:T(128)S(1)}, f32[128]{0:T(128)}, u32[]{:S(2)}) copy-start(f32[128]{0:T(128)} %copy-done.64) | copy-start | bytes 1540
  177.8 29.1 %copy-start.20 = (f32[256,1]{0,1:T(1,128)S(1)}, f32[256,1]{0,1:T(1,128)}, u32[]{:S(2)}) copy-start(f32[256,1]{0,1:T(1,128)} %copy-done.19) | copy-start | bytes 3076
  177.8 29.1 %copy-start.22 = (f32[256,1]{0,1:T(1,128)S(1)}, f32[256,1]{0,1:T(1,128)}, u32[]{:S(2)}) copy-start(f32[256,1]{0,1:T(1,128)} %copy-done.21) | copy-start | bytes 3076
  177.8 29.1 %copy-start.24 = (f32[256,1]{0,1:T(1,128)S(1)}, f32[256,1]{0,1:T(1,128)}, u32[]{:S(2)}) copy-start(f32[256,1]{0,1:T(1,128)} %copy-done.23) | copy-start | bytes 3076
  177.8 29.1 %copy-start.26 = (f32[256,1]{0,1:T(1,128)S(1)}, f32[256,1]{0,1:T(1,128)}, u32[]{:S(2)}) copy-start(f32[256,1]{0,1:T(1,128)} %copy-done.25) | copy-start | bytes 3076
  177.9 29.1 %copy-start.28 = (f32[256,1]{0,1:T(1,128)S(1)}, f32[256,1]{0,1:T(1,128)}, u32[]{:S(2)}) copy-start(f32[256,1]{0,1:T(1,128)} %copy-done.27) | copy-start | bytes 3076
  177.9 29.1 %copy-start.30 = (f32[256,1]{0,1:T(1,128)S(1)}, f32[256,1]{0,1:T(1,128)}, u32[]{:S(2)}) copy-start(f32[256,1]{0,1:T(1,128)} %copy-done.29) | copy-start | bytes 3076
  177.9 29.1 %copy-start.32 = (f32[256,1]{0,1:T(1,128)S(1)}, f32[256,1]{0,1:T(1,128)}, u32[]{:S(2)}) copy-start(f32[256,1]{0,1:T(1,128)} %copy-done.31) | copy-start | bytes 3076
  177.9 29.1 %copy-start.34 = (f32[256,1]{0,1:T(1,128)S(1)}, f32[256,1]{0,1:T(1,128)}, u32[]{:S(2)}) copy-start(f32[256,1]{0,1:T(1,128)} %copy-done.33) | copy-start | bytes 3076
  177.9 29.1 %copy-start.36 = (f32[256,1]{0,1:T(1,128)S(1)}, f32[256,1]{0,1:T(1,128)}, u32[]{:S(2)}) copy-start(f32[256,1]{0,1:T(1,128)} %copy-done.35) | copy-start | bytes 3076
  177.9 29.1 %copy-start.38 = (f32[256,1]{0,1:T(1,128)S(1)}, f32[256,1]{0,1:T(1,128)}, u32[]{:S(2)}) copy-start(f32[256,1]{0,1:T(1,128)} %copy-done.37) | copy-start | bytes 3076
  177.9 29.1 %copy-start.40 = (f32[256,1]{0,1:T(1,128)S(1)}, f32[256,1]{0,1:T(1,128)}, u32[]{:S(2)}) copy-start(f32[256,1]{0,1:T(1,128)} %copy-done.39) | copy-start | bytes 3076
  177.9 29.1 %copy-start.42 = (f32[256,1]{0,1:T(1,128)S(1)}, f32[256,1]{0,1:T(1,128)}, u32[]{:S(2)}) copy-start(f32[256,1]{0,1:T(1,128)} %copy-done.41) | copy-start | bytes 3076
  177.9 29.1 %copy-start.44 = (f32[256,1]{0,1:T(1,128)S(1)}, f32[256,1]{0,1:T(1,128)}, u32[]{:S(2)}) copy-start(f32[256,1]{0,1:T(1,128)} %copy-done.43) | copy-start | bytes 3076
  177.9 29.1 %copy-start.46 = (f32[256,1]{0,1:T(1,128)S(1)}, f32[256,1]{0,1:T(1,128)}, u32[]{:S(2)}) copy-start(f32[256,1]{0,1:T(1,128)} %copy-done.45) | copy-start | bytes 3076
  178.0 29.1 %copy-start.48 = (f32[256,1]{0,1:T(1,128)S(1)}, f32[256,1]{0,1:T(1,128)}, u32[]{:S(2)}) copy-start(f32[256,1]{0,1:T(1,128)} %copy-done.47) | copy-start | bytes 3076
  178.0 29.1 %copy-start.50 = (f32[256,1]{0,1:T(1,128)S(1)}, f32[256,1]{0,1:T(1,128)}, u32[]{:S(2)}) copy-start(f32[256,1]{0,1:T(1,128)} %copy-done.49) | copy-start | bytes 3076
  178.0 29.1 %copy-start.52 = (f32[256,1]{0,1:T(1,128)S(1)}, f32[256,1]{0,1:T(1,128)}, u32[]{:S(2)}) copy-start(f32[256,1]{0,1:T(1,128)} %copy-done.51) | copy-start | bytes 3076
  178.0 29.1 %copy-start.54 = (f32[256,1]{0,1:T(1,128)S(1)}, f32[256,1]{0,1:T(1,128)}, u32[]{:S(2)}) copy-start(f32[256,1]{0,1:T(1,128)} %copy-done.53) | copy-start | bytes 3076
  178.0 29.1 %copy-start.56 = (f32[256,1]{0,1:T(1,128)S(1)}, f32[256,1]{0,1:T(1,128)}, u32[]{:S(2)}) copy-start(f32[256,1]{0,1:T(1,128)} %copy-done.55) | copy-start | bytes 3076
  178.0 29.1 %copy-start.58 = (f32[256,1]{0,1:T(1,128)S(1)}, f32[256,1]{0,1:T(1,128)}, u32[]{:S(2)}) copy-start(f32[256,1]{0,1:T(1,128)} %copy-done.57) | copy-start | bytes 3076
  178.0 29.1 %copy-start.60 = (f32[256,1]{0,1:T(1,128)S(1)}, f32[256,1]{0,1:T(1,128)}, u32[]{:S(2)}) copy-start(f32[256,1]{0,1:T(1,128)} %copy-done.59) | copy-start | bytes 3076
  179.5 27.5 %collective-permute-start.9 = (bf16[256,15]{0,1:T(8,128)(2,1)S(1)}, bf16[256,15]{0,1:T(8,128)(2,1)S(1)}, u32[]{:S(2)}, u32[]{:S(2)}) collective-permute-start(bf16[256,15]{0,1:T(8,128)(2,1)S(1)} %get-tuple-element.76), channel_id=1, source_target_pairs={{0,4},{4,8},{8,12},{12,16},{16,20},{20,24},{24,28},{28,0},{1,5},{5... | collective-permute-start | bytes 23048 | tf_op jit(solution)/shard_map/ppermute | solution.py:32
  179.5 27.4 %collective-permute-start.10 = (bf16[256,15]{0,1:T(8,128)(2,1)S(1)}, bf16[256,15]{0,1:T(8,128)(2,1)S(1)}, u32[]{:S(2)}, u32[]{:S(2)}) collective-permute-start(bf16[256,15]{0,1:T(8,128)(2,1)S(1)} %get-tuple-element.77), channel_id=1, source_target_pairs={{4,0},{8,4},{12,8},{16,12},{20,16},{24,20},{28,24},{0,28},{5,1},{9... | collective-permute-start | bytes 23048 | tf_op jit(solution)/shard_map/ppermute | solution.py:34
  (18 other events, 15.0 us)
Sparse Core Ops, SparseCore 0:
  121.0 18.2 reduce-scatter.2
  141.7 17.8 reduce-scatter.4
